TPU v7x, 512 devices: a whole 4x8x8 slice. The times are simulated.
512 devices in a mesh: sector: 32 (over y, x), term: 16 (over z, core).
Axes of the slice: x: 4, y: 8, z: 8, core: 2. Of those that a mesh axis runs over, the one named last changes fastest.
Arguments:
- wavefunction: bfloat16 [64, 256, 256], P('sector', 'term'), as said below
- sector_sizes: int32 [64, 2], P('sector'), may hold values from 64 to 256, as said below
- term_shifts: int32 [128], P('term'), may hold values from -2 to 2
- left_blocks: bfloat16 [128, 64, 256, 256], P('term', 'sector')
- right_blocks: bfloat16 [128, 64, 256, 256], P('term', 'sector')
Outputs:
- sigma: float32 [64, 256, 256], P('sector', 'term')
- sigma_next: float32 [64, 256, 256], P('sector', 'term')
Inputs may be any that keep to these rules, and one draw needn't show every extreme that they name: `sector_sizes`: in every draw one sector has 256 live rows and columns and another has 64 of both. `wavefunction`: entries outside a sector's live rows and columns are arbitrary.
All inputs are finite; a program needn't handle non-finite values.
Results may differ from a plain program's by a relative error of at most 0.0045.
Values may be sent and summed in bfloat16 or wider, within the bound.
A program may use at most 64 MiB of HBM per device.

v0:
```python
import jax
import jax.numpy as jnp
from jax import lax
from jax.sharding import PartitionSpec as P

H = 2


def padded(value, sides, width):
    for axis, dim in sides:
        size, length = (lax.axis_size(axis), value.shape[dim])
        up = [(i, (i + 1) % size) for i in range(size - 1)]
        down = [(j, i) for i, j in up]
        last = lax.slice_in_dim(value, length - width, length, axis=dim)
        first = lax.slice_in_dim(value, 0, width, axis=dim)
        before = lax.ppermute(last, axis, up)
        after = lax.ppermute(first, axis, down)
        value = jnp.concatenate([before, value, after], axis=dim)
    return value


def sector_mask(sector_sizes, width):
    index = jnp.arange(width, dtype=jnp.int32)
    rows_live = index[None, :, None] < sector_sizes[:, 0][:, None, None]
    cols_live = index[None, None, :] < sector_sizes[:, 1][:, None, None]
    return (rows_live & cols_live).astype(jnp.float32)


def term_total(left, right, sources):
    mixed = jnp.einsum("tij,tjk->tik", left, sources, preferred_element_type=jnp.float32).astype(
        jnp.bfloat16
    )
    return jnp.einsum("tik,tlk->il", mixed, right, preferred_element_type=jnp.float32)


def apply_hamiltonian(block, term_shifts, left_blocks, right_blocks, live):
    nearby = padded(block, (("sector", 0),), H)
    results = []
    for sector_idx in range(block.shape[0]):
        source = sector_idx + H - term_shifts
        sources = jnp.take(nearby, source, axis=0)
        left = left_blocks[:, sector_idx]
        right = right_blocks[:, sector_idx]
        total = term_total(left, right, sources)
        results.append(total)
    return jnp.stack(results, axis=0) * live


def on_device(wavefunction, sector_sizes, term_shifts, left_blocks, right_blocks):
    width = left_blocks.shape[2]
    row_count = wavefunction.shape[1]
    row_start = lax.axis_index("term") * row_count
    live = sector_mask(sector_sizes, width)
    own_live = lax.dynamic_slice_in_dim(live, row_start, row_count, 1)
    psi_own = (wavefunction.astype(jnp.float32) * own_live).astype(jnp.bfloat16)
    block = lax.all_gather(psi_own, "term", axis=1, tiled=True)
    first = apply_hamiltonian(block, term_shifts, left_blocks, right_blocks, live)
    sigma_own = lax.psum_scatter(first, "term", scatter_dimension=1, tiled=True)
    psi_wide = psi_own.astype(jnp.float32)
    numerator, denominator = lax.psum(
        (jnp.sum(psi_wide * sigma_own), jnp.sum(psi_wide * psi_wide)), ("sector", "term")
    )
    theta = numerator / denominator
    residual_own = (sigma_own - theta * psi_wide).astype(jnp.bfloat16)
    residual = lax.all_gather(residual_own, "term", axis=1, tiled=True)
    second = apply_hamiltonian(residual, term_shifts, left_blocks, right_blocks, live)
    sigma_next = lax.psum_scatter(second, "term", scatter_dimension=1, tiled=True)
    return (sigma_own, sigma_next)


def solution(mesh):
    return jax.shard_map(
        on_device,
        mesh=mesh,
        in_specs=(
            P("sector", "term", None),
            P("sector", None),
            P("term"),
            P("term", "sector", None, None),
            P("term", "sector", None, None),
        ),
        out_specs=(P("sector", "term", None), P("sector", "term", None)),
        check_vma=False,
    )
```

profile of v0, /device:TPU:7, one launch (start us, length us, event | category | flops | bytes accessed | tf_op | source)
XLA Modules:
  0.0 315.8 jit_solution(8790842931723353120)
XLA Ops:
  7.2 1.0 slice_reduce_fusion.1
  8.4 0.7 multiply_convert_fusion
  9.1 24.4 %all_gather.6 = bf16[2,256,256]{2,1,0:T(8,128)(2,1)S(1)} all-gather(bf16[2,16,256]{2,1,0:T(8,128)(2,1)S(1)} %multiply_convert_fusion), channel_id=1, replica_groups=mesh['sector'=32,'term'=16] {'term'}, dimensions={1}, use_global_device_ids=true | all-gather | bytes 278528 | tf_op jit(solution)/shard_map/all_gather | solution.py:56
  33.5 3.1 collective-permute-start
  36.6 2.2 collective-permute-start.1
  38.8 0.7 compare_and_fusion.1
  39.5 3.7 %collective-permute-done = bf16[2,256,256]{2,1,0:T(8,128)(2,1)S(1)} collective-permute-done((bf16[2,256,256]{2,1,0:T(8,128)(2,1)S(1)}, bf16[2,256,256]{2,1,0:T(8,128)(2,1)S(1)}, u32[]{:S(2)}, u32[]{:S(2)}) %collective-permute-start) | collective-permute-done | bytes 262176 | tf_op jit(solution)/shard_map/ppermute | solution.py:16
  43.2 4.9 %collective-permute-done.1 = bf16[2,256,256]{2,1,0:T(8,128)(2,1)S(1)} collective-permute-done((bf16[2,256,256]{2,1,0:T(8,128)(2,1)S(1)}, bf16[2,256,256]{2,1,0:T(8,128)(2,1)S(1)}, u32[]{:S(2)}, u32[]{:S(2)}) %collective-permute-start.1) | collective-permute-done | bytes 262176 | tf_op jit(solution)/shard_map/ppermute | solution.py:17
  49.3 2.4 fusion.8
  51.8 2.4 fusion.9
  54.2 0.9 maximum_select_fusion
  55.2 54.7 %reduce-scatter.3.cloned.1.call-done = f32[2,16,256]{2,1,0:T(8,128)} async-done(((f32[2,256,256]{2,1,0:T(8,128)}), f32[2,16,256]{2,1,0:T(8,128)}) %reduce-scatter.3.cloned.1.call-update) | async-done | bytes 32784 | tf_op jit(solution)/shard_map/reduce_scatter | solution.py:58
  110.0 1.5 fusion.61
  111.4 98.0 %all-reduce = (f32[]{:T(128)}, f32[]{:T(128)}) all-reduce(f32[]{:T(128)} %get-tuple-element.4, f32[]{:T(128)} %get-tuple-element.3), channel_id=1, replica_groups=mesh['sector'=32,'term'=16] {'sector','term'}, use_global_device_ids=true, to_apply=%region_2.4 | all-reduce | flops 2 | bytes 16 | tf_op jit(solution)/shard_map/psum | solution.py:60
  210.7 0.8 fusion.63
  211.4 17.1 %all_gather.7 = bf16[2,256,256]{2,1,0:T(8,128)(2,1)S(1)} all-gather(bf16[2,16,256]{2,1,0:T(8,128)(2,1)S(1)} %fusion.63), channel_id=1, replica_groups=mesh['sector'=32,'term'=16] {'term'}, dimensions={1}, use_global_device_ids=true | all-gather | bytes 278528 | tf_op jit(solution)/shard_map/all_gather | solution.py:65
  228.6 3.6 %collective-permute-start.2 = (bf16[2,256,256]{2,1,0:T(8,128)(2,1)S(1)}, bf16[2,256,256]{2,1,0:T(8,128)(2,1)S(1)}, u32[]{:S(2)}, u32[]{:S(2)}) collective-permute-start(bf16[2,256,256]{2,1,0:T(8,128)(2,1)S(1)} %all_gather.7), channel_id=1, source_target_pairs={{0,16},{16,32},{32,48},{48,64},{64,80},{80,96},{96,112},{112,128},... | collective-permute-start | bytes 786440 | tf_op jit(solution)/shard_map/ppermute | solution.py:16
  232.2 1.9 collective-permute-start.3
  234.1 4.1 %collective-permute-done.2 = bf16[2,256,256]{2,1,0:T(8,128)(2,1)S(1)} collective-permute-done((bf16[2,256,256]{2,1,0:T(8,128)(2,1)S(1)}, bf16[2,256,256]{2,1,0:T(8,128)(2,1)S(1)}, u32[]{:S(2)}, u32[]{:S(2)}) %collective-permute-start.2) | collective-permute-done | bytes 262176 | tf_op jit(solution)/shard_map/ppermute | solution.py:16
  238.3 5.4 %collective-permute-done.3 = bf16[2,256,256]{2,1,0:T(8,128)(2,1)S(1)} collective-permute-done((bf16[2,256,256]{2,1,0:T(8,128)(2,1)S(1)}, bf16[2,256,256]{2,1,0:T(8,128)(2,1)S(1)}, u32[]{:S(2)}, u32[]{:S(2)}) %collective-permute-start.3) | collective-permute-done | bytes 262176 | tf_op jit(solution)/shard_map/ppermute | solution.py:17
  244.9 2.4 fusion.10
  247.4 2.4 fusion.11
  249.8 0.9 maximum_select_fusion.1
  250.8 58.2 %reduce-scatter.5.cloned.1.call-done = f32[2,16,256]{2,1,0:T(8,128)} async-done(((f32[2,256,256]{2,1,0:T(8,128)}), f32[2,16,256]{2,1,0:T(8,128)}) %reduce-scatter.5.cloned.1.call-update) | async-done | bytes 32784 | tf_op jit(solution)/shard_map/reduce_scatter | solution.py:67
  (17 shorter events, 2.9 us)
Async XLA Ops:
  7.2 102.8 %reduce-scatter.3.cloned.1.call-start = ((), (), s32[]{:S(2)}) async-start(), calls=%async_computation.2 | async-start | bytes 557056 | tf_op jit(solution)/shard_map/reduce_scatter | solution.py:58
  33.5 9.6 %collective-permute-start = (bf16[2,256,256]{2,1,0:T(8,128)(2,1)S(1)}, bf16[2,256,256]{2,1,0:T(8,128)(2,1)S(1)}, u32[]{:S(2)}, u32[]{:S(2)}) collective-permute-start(bf16[2,256,256]{2,1,0:T(8,128)(2,1)S(1)} %all_gather.6), channel_id=1, source_target_pairs={{0,16},{16,32},{32,48},{48,64},{64,80},{80,96},{96,112},{112,128},... | collective-permute-start | bytes 786440 | tf_op jit(solution)/shard_map/ppermute | solution.py:16
  36.6 11.4 %collective-permute-start.1 = (bf16[2,256,256]{2,1,0:T(8,128)(2,1)S(1)}, bf16[2,256,256]{2,1,0:T(8,128)(2,1)S(1)}, u32[]{:S(2)}, u32[]{:S(2)}) collective-permute-start(bf16[2,256,256]{2,1,0:T(8,128)(2,1)S(1)} %all_gather.6), channel_id=1, source_target_pairs={{16,0},{32,16},{48,32},{64,48},{80,64},{96,80},{112,96},{128,112},... | collective-permute-start | bytes 786440 | tf_op jit(solution)/shard_map/ppermute | solution.py:17
  55.2 253.8 %reduce-scatter.5.cloned.1.call-start = ((), (), s32[]{:S(2)}) async-start(), calls=%async_computation.3 | async-start | bytes 557056 | tf_op jit(solution)/shard_map/reduce_scatter | solution.py:67
  228.6 9.6 %collective-permute-start.2 = (bf16[2,256,256]{2,1,0:T(8,128)(2,1)S(1)}, bf16[2,256,256]{2,1,0:T(8,128)(2,1)S(1)}, u32[]{:S(2)}, u32[]{:S(2)}) collective-permute-start(bf16[2,256,256]{2,1,0:T(8,128)(2,1)S(1)} %all_gather.7), channel_id=1, source_target_pairs={{0,16},{16,32},{32,48},{48,64},{64,80},{80,96},{96,112},{112,128},... | collective-permute-start | bytes 786440 | tf_op jit(solution)/shard_map/ppermute | solution.py:16
  232.2 11.4 %collective-permute-start.3 = (bf16[2,256,256]{2,1,0:T(8,128)(2,1)S(1)}, bf16[2,256,256]{2,1,0:T(8,128)(2,1)S(1)}, u32[]{:S(2)}, u32[]{:S(2)}) collective-permute-start(bf16[2,256,256]{2,1,0:T(8,128)(2,1)S(1)} %all_gather.7), channel_id=1, source_target_pairs={{16,0},{32,16},{48,32},{64,48},{80,64},{96,80},{112,96},{128,112},... | collective-permute-start | bytes 786440 | tf_op jit(solution)/shard_map/ppermute | solution.py:17
Sparse Core Ops, SparseCore 0:
  55.3 54.6 reduce-scatter.2
  250.9 58.0 reduce-scatter.4
where the time goes:
time: 319 us; the launch traced here: 316 us
  blocking collectives  139 us (44%)
  waiting for transfers between devices  131 us (41%)
  between operations  15.4 us (5%)
  starting transfers between devices  10.9 us (3%)
  matrix products  9.79 us (3%)
  other arithmetic  5.7 us (2%)
  local copies, waits for them, and re-layouts  3.53 us (1%)
    psum x1, blocking collectives, on_device(): lax.psum((jnp.sum(psi_wide * sigma_own), jnp.sum(psi_wide * psi_wide)), (...  98 us
    reduce_scatter x1, waiting for transfers between devices, on_device(): lax.psum_scatter(second, 'term', scatter_dimension=1, tiled=True)  58.2 us
    reduce_scatter x1, waiting for transfers between devices, on_device(): sigma_own = lax.psum_scatter(first, 'term', scatter_dimension=1, tiled=True)  54.7 us
    all_gather x1, blocking collectives, on_device(): block = lax.all_gather(psi_own, 'term', axis=1, tiled=True)  24.4 us
    all_gather x1, blocking collectives, on_device(): residual = lax.all_gather(residual_own, 'term', axis=1, tiled=True)  17.1 us
    ppermute x2, waiting for transfers between devices, padded(): after = lax.ppermute(first, axis, down)  10.3 us
    dot_general x4, matrix products, term_total(): jnp.einsum('tik,tlk->il', mixed, right, preferred_element_type=jnp.float32)  9.79 us
    ppermute x2, waiting for transfers between devices, padded(): before = lax.ppermute(last, axis, up)  7.75 us
  transfers between devices with their start and end apart: 6, of which 6 were waited for; matrix products, arithmetic and copies ran while one was open for 0% of the time, Pallas kernels for 0%

commit v1 on v0

v1 whole, which is shorter than its diff:
```python
import functools

import jax
import jax.numpy as jnp
from jax import lax
from jax.experimental import pallas as pl
from jax.experimental.pallas import tpu as pltpu
from jax.sharding import PartitionSpec as P

H = 2
MESH = pl.DeviceIdType.MESH
F32, BF16 = jnp.float32, jnp.bfloat16
INNER = 4


class Sems:
    def __init__(self, send, recv):
        self.send, self.recv, self.count = send, recv, 0

    def take(self):
        self.count += 1
        return self.count - 1


def kernel(
    dims, psi_ref, sizes_ref, shifts_ref, left_hbm, right_hbm, sigma_ref, next_ref,
    left, right, v0, v1, mixed, total, peer, chunk, landed, th_own, th_z, th_x, th_y,
    load_sem, send_sem, recv_sem,
):
    n_sector, n_term = dims
    nz = n_term // 2
    n_outer = n_sector // INNER
    terms, width = left.shape[0], left.shape[-1]
    rows = psi_ref.shape[1]
    s, t = lax.axis_index("sector"), lax.axis_index("term")
    z, c = t // 2, t % 2
    sx, sy = s % INNER, s // INNER
    other = 1 - c
    has_lo, has_hi = s > 0, s < n_sector - 1
    sems = Sems(send_sem, recv_sem)
    sent = []

    def at_z(d):
        return lax.rem(z + d, nz)

    def dev(sector, zz, core):
        return (sector, zz * 2 + core)

    def remote(src, dst, idx, device):
        return pltpu.make_async_remote_copy(
            src_ref=src, dst_ref=dst, send_sem=send_sem.at[idx], recv_sem=recv_sem.at[idx],
            device_id=device, device_id_type=MESH,
        )

    def send(src, dst, idx, device, when=None):
        copy = remote(src, dst, idx, device)
        if when is None:
            copy.start()
        else:
            pl.when(when)(copy.start)
        sent.append((copy, when))

    def arrive(dst, idx, when=None):
        copy = remote(dst, dst, idx, dev(s, z, other))
        if when is None:
            copy.wait_recv()
        else:
            pl.when(when)(copy.wait_recv)

    loads = []
    loads.append(pltpu.make_async_copy(left_hbm, left, load_sem.at[0]))
    for k in range(terms):
        for i in range(2):
            loads.append(
                pltpu.make_async_copy(
                    right_hbm.at[k, i], right.at[i, :, pl.ds(k * width, width)],
                    load_sem.at[1 + 2 * k + i],
                )
            )
    for load in loads:
        load.start()

    barrier = pltpu.get_barrier_semaphore()

    def greet(device):
        pl.semaphore_signal(barrier, inc=1, device_id=device, device_id_type=MESH)

    greet(dev(s, z, other))
    for d in range(1, nz):
        greet(dev(s, at_z(d), c))
    for d in range(1, INNER):
        greet(dev(sy * INNER + lax.rem(sx + d, INNER), z, c))
    for d in range(1, n_outer):
        greet(dev(lax.rem(sy + d, n_outer) * INNER + sx, z, c))
    lo_cross = jnp.logical_and(has_lo, sx == 0)
    hi_cross = jnp.logical_and(has_hi, sx == INNER - 1)
    pl.when(lo_cross)(lambda: greet(dev(s - 1, z, c)))
    pl.when(hi_cross)(lambda: greet(dev(s + 1, z, c)))

    def live(i):
        row = lax.broadcasted_iota(jnp.int32, (rows, width), 0) + t * rows
        col = lax.broadcasted_iota(jnp.int32, (rows, width), 1)
        return jnp.logical_and(row < sizes_ref[i, 0], col < sizes_ref[i, 1])

    lives = [live(i) for i in range(2)]
    squares = jnp.zeros((8, 128), F32)

    def fold(x):
        x = x.reshape(-1, 8, width).sum(axis=0)
        return functools.reduce(jnp.add, [x[:, k : k + 128] for k in range(0, width, 128)])

    for i in range(2):
        own = jnp.where(lives[i], psi_ref[i].astype(F32), 0.0)
        v0[2 + i, z, c] = own.astype(BF16)
        squares += fold(own * own)

    @pl.when(jnp.logical_not(has_lo))
    def _():
        v0[0:2] = jnp.zeros((2, nz, 2, rows, width), BF16)
        v1[0:2] = jnp.zeros((2, nz, 2, rows, width), BF16)

    @pl.when(jnp.logical_not(has_hi))
    def _():
        v0[4:6] = jnp.zeros((2, nz, 2, rows, width), BF16)
        v1[4:6] = jnp.zeros((2, nz, 2, rows, width), BF16)

    pl.semaphore_wait(
        barrier,
        1 + (nz - 1) + (INNER - 1) + (n_outer - 1)
        + lo_cross.astype(jnp.int32) + hi_cross.astype(jnp.int32),
    )

    order = []
    for d in range(1, nz // 2 + 1):
        order.append(d)
        if nz - d != d:
            order.append(nz - d)

    def gather(v):
        zi = [sems.take() for _ in range(nz)]
        lo = [sems.take() for _ in range(nz)]
        hi = [sems.take() for _ in range(nz)]
        sib = [sems.take() for _ in range(3)]
        mid = pl.ds(2, 2)
        for d in order:
            send(v.at[mid, z, c], v.at[mid, z, c], zi[d], dev(s, at_z(d), c))
        for d in [0] + order:
            zz = at_z(nz - d) if d else z
            block = v.at[mid, zz, c]
            if d:
                arrive(block, zi[d])
            send(block, v.at[pl.ds(4, 2), zz, c], lo[d], dev(s - 1, z, c), has_lo)
            send(block, v.at[pl.ds(0, 2), zz, c], hi[d], dev(s + 1, z, c), has_hi)
        whole = [v.at[pl.ds(2 * k, 2), :, c] for k in range(3)]
        back = [v.at[pl.ds(2 * k, 2), :, other] for k in range(3)]
        send(whole[1], whole[1], sib[1], dev(s, z, other))
        for d in [0] + order:
            zz = at_z(nz - d) if d else z
            arrive(v.at[pl.ds(0, 2), zz, c], hi[d], has_lo)
            arrive(v.at[pl.ds(4, 2), zz, c], lo[d], has_hi)
        send(whole[0], whole[0], sib[0], dev(s, z, other), has_lo)
        send(whole[2], whole[2], sib[2], dev(s, z, other), has_hi)
        arrive(back[1], sib[1])
        arrive(back[0], sib[0], has_lo)
        arrive(back[2], sib[2], has_hi)

    def first_half(v, i):
        for k in range(terms):
            block = v[i + H - shifts_ref[k]].reshape(width, width)
            out = jnp.dot(left[k, i], block, preferred_element_type=F32)
            mixed[:, k * width : (k + 1) * width] = out.astype(BF16)

    def second_half(r, i):
        out = lax.dot_general(
            mixed[...], right[i], (((1,), (1,)), ((), ())), preferred_element_type=F32
        )
        total[r, i] = out.reshape(nz, 2, rows, width)
        return out

    def swap(r, i, idx):
        send(total.at[r, i, :, other], peer.at[r, i], idx, dev(s, z, other))

    def scatter(r, i, idx, zi):
        arrive(peer.at[r, i], idx)
        chunk[r, i] = (total[r, i, :, c] + peer[r, i]).astype(chunk.dtype)
        for d in order:
            zz = at_z(d)
            send(chunk.at[r, i, zz], landed.at[r, i, z], zi[d], dev(s, zz, c))

    def collect(r, i, zi):
        acc = total[r, i, z, c] + peer[r, i, z]
        for d in order:
            zz = at_z(nz - d)
            arrive(landed.at[r, i, zz], zi[d])
            acc = acc + landed[r, i, zz].astype(F32)
        return jnp.where(lives[i], acc, 0.0)

    def product(r, v):
        gather(v)
        swaps = [sems.take() for _ in range(2)]
        zis = [[sems.take() for _ in range(nz)] for _ in range(2)]
        if r == 0:
            for load in loads:
                load.wait()
        outs = []
        first_half(v, 0)
        outs.append(second_half(r, 0))
        swap(r, 0, swaps[0])
        inner = fold(outs[0] * v0[2].reshape(width, width).astype(F32)) if r == 0 else None
        first_half(v, 1)
        scatter(r, 0, swaps[0], zis[0])
        outs.append(second_half(r, 1))
        swap(r, 1, swaps[1])
        if r == 0:
            inner += fold(outs[1] * v0[3].reshape(width, width).astype(F32))
            theta_start(inner)
        scatter(r, 1, swaps[1], zis[1])
        theta = theta_end() if r == 0 else None
        return [collect(r, i, zis[i]) for i in range(2)], theta

    tz = [sems.take() for _ in range(n_term)]
    tx = [sems.take() for _ in range(INNER)]
    ty = [sems.take() for _ in range(n_outer)]

    def theta_start(inner):
        th_own[0] = jnp.concatenate([inner[:4] + inner[4:], squares[:4] + squares[4:]], axis=0)
        for d in range(1, n_term):
            send(th_own.at[0], th_z.at[d], tz[d], (s, lax.rem(t + d, n_term)))

    def theta_end():
        def summed(own, slots, idx, n):
            acc = own
            for d in range(1, n):
                arrive(slots.at[d], idx[d])
                acc = acc + slots[d]
            return acc

        th_own[1] = summed(th_own[0], th_z, tz, n_term)
        for d in range(1, INNER):
            send(th_own.at[1], th_x.at[d], tx[d], (sy * INNER + lax.rem(sx + d, INNER), t))
        th_own[2] = summed(th_own[1], th_x, tx, INNER)
        for d in range(1, n_outer):
            send(th_own.at[2], th_y.at[d], ty[d], (lax.rem(sy + d, n_outer) * INNER + sx, t))
        both = summed(th_own[2], th_y, ty, n_outer)
        num = jnp.sum(both[:4], keepdims=True)
        den = jnp.sum(both[4:], keepdims=True)
        return num / den

    sigma, theta = product(0, v0)
    for i in range(2):
        sigma_ref[i] = sigma[i]
        psi = v0[2 + i, z, c].astype(F32)
        v1[2 + i, z, c] = (sigma[i] - theta * psi).astype(BF16)
    last, _ = product(1, v1)
    for i in range(2):
        next_ref[i] = last[i]
    for copy, when in sent:
        if when is None:
            copy.wait_send()
        else:
            pl.when(when)(copy.wait_send)
    assert sems.count <= send_sem.shape[0]


def solution(mesh, link=BF16):
    dims = (mesh.shape["sector"], mesh.shape["term"])

    def step(psi, sizes, shifts, left, right):
        n_sector, n_term = dims
        nz = n_term // 2
        terms, width, rows = left.shape[0], left.shape[-1], psi.shape[1]
        n_sems = 2 * (3 * nz + 3 + 2 + 2 * nz) + n_term + INNER + n_sector // INNER
        out = jax.ShapeDtypeStruct((2, rows, width), F32)
        vmem, smem = (pl.BlockSpec(memory_space=m) for m in (pltpu.VMEM, pltpu.SMEM))
        hbm = pl.BlockSpec(memory_space=pl.ANY)
        return pl.pallas_call(
            functools.partial(kernel, dims),
            out_shape=(out, out),
            in_specs=[vmem, smem, smem, hbm, hbm],
            out_specs=(vmem, vmem),
            scratch_shapes=[
                pltpu.VMEM((terms, 2, width, width), BF16),
                pltpu.VMEM((2, width, terms * width), BF16),
                pltpu.VMEM((6, nz, 2, rows, width), BF16),
                pltpu.VMEM((6, nz, 2, rows, width), BF16),
                pltpu.VMEM((width, terms * width), BF16),
                pltpu.VMEM((2, 2, nz, 2, rows, width), F32),
                pltpu.VMEM((2, 2, nz, rows, width), F32),
                pltpu.VMEM((2, 2, nz, rows, width), link),
                pltpu.VMEM((2, 2, nz, rows, width), link),
                pltpu.VMEM((3, 8, 128), F32),
                pltpu.VMEM((n_term, 8, 128), F32),
                pltpu.VMEM((INNER, 8, 128), F32),
                pltpu.VMEM((n_sector // INNER, 8, 128), F32),
                pltpu.SemaphoreType.DMA((1 + 2 * terms,)),
                pltpu.SemaphoreType.DMA((n_sems,)),
                pltpu.SemaphoreType.DMA((n_sems,)),
            ],
            compiler_params=pltpu.CompilerParams(
                collective_id=0, has_side_effects=True, vmem_limit_bytes=62 * 2**20
            ),
            cost_estimate=pl.CostEstimate(
                flops=8 * terms * width**3 * 2, bytes_accessed=4 * terms * width * width * 2,
                transcendentals=0,
            ),
        )(psi, sizes, shifts, left, right)

    return jax.shard_map(
        step,
        mesh=mesh,
        in_specs=(
            P("sector", "term", None),
            P("sector", None),
            P("term"),
            P("term", "sector", None, None),
            P("term", "sector", None, None),
        ),
        out_specs=(P("sector", "term", None), P("sector", "term", None)),
        check_vma=False,
    )
```

time: 319 us -> 69.8 us (0.22)
  the two profiles are of different devices: /device:TPU:7 before, /device:TPU:9 now
where the time goes in v1:
time: 69.8 us; the launch traced here: 69.5 us
  Pallas kernels  66.1 us (95%)
  local copies, waits for them, and re-layouts  2.75 us (4%)
    pallas_call x1, Pallas kernels, step(): pl.pallas_call(functools.partial(kernel, dims), out_shape=(out, out), in_...  66.1 us
    unnamed x2, local copies, waits for them, and re-layouts  2.75 us

profile of v1, /device:TPU:9, one launch (start us, length us, event | category | flops | bytes accessed | tf_op | source)
XLA Modules:
  0.0 69.5 jit_solution(14958769019382473943)
XLA Ops:
  0.6 66.1 %shard_map.68 = (f32[2,16,256]{2,1,0:T(8,128)}, f32[2,16,256]{2,1,0:T(8,128)}) custom-call(bf16[2,16,256]{2,1,0:T(8,128)(2,1)} %psi_ref.1, s32[2,2]{1,0:T(2,128)} %sizes_ref.1, s32[8]{0:T(128)} %shifts_ref.1, bf16[8,2,256,256]{3,2,1,0:T(8,128)(2,1)} %left_hbm.1, bf16[8,2,256,256]{3,2,1,0:T(8,128)(2,1)} %right_hbm.1), custom_call_target="tpu_custom_call" | custom-call | flops 2147483648 | bytes 4194304 | tf_op jit(solution)/shard_map/pallas_call | solution.py:276
  66.7 1.4 %copy.9 = f32[2,16,256]{2,1,0:T(8,128)} copy(f32[2,16,256]{2,1,0:T(8,128)} %get-tuple-element.4) | data formatting | bytes 65536
  68.1 1.4 %copy.10 = f32[2,16,256]{2,1,0:T(8,128)} copy(f32[2,16,256]{2,1,0:T(8,128)} %get-tuple-element.5) | data formatting | bytes 65536

commit v2 on v1

--- a/solution.py
+++ b/solution.py
@@ -23,9 +23,9 @@
 
 
 def kernel(
-    dims, psi_ref, sizes_ref, shifts_ref, left_hbm, right_hbm, sigma_ref, next_ref,
-    left, right, v0, v1, mixed, total, peer, chunk, landed, th_own, th_z, th_x, th_y,
-    load_sem, send_sem, recv_sem,
+    dims, psi_hbm, sizes_ref, shifts_ref, left_hbm, right_hbm, sigma_hbm, next_hbm,
+    psi_ref, outs, left, right, v0, v1, v2, mixed, total, peer, chunk, landed,
+    th_own, th_z, th_x, th_y, th_side, load_sem, send_sem, recv_sem,
 ):
     n_sector, n_term = dims
     nz = n_term // 2
@@ -67,14 +67,16 @@
         else:
             pl.when(when)(copy.wait_recv)
 
+    own_load = pltpu.make_async_copy(psi_hbm, psi_ref, load_sem.at[0])
+    own_load.start()
     loads = []
-    loads.append(pltpu.make_async_copy(left_hbm, left, load_sem.at[0]))
+    loads.append(pltpu.make_async_copy(left_hbm, left, load_sem.at[1]))
     for k in range(terms):
         for i in range(2):
             loads.append(
                 pltpu.make_async_copy(
                     right_hbm.at[k, i], right.at[i, :, pl.ds(k * width, width)],
-                    load_sem.at[1 + 2 * k + i],
+                    load_sem.at[2 + 2 * k + i],
                 )
             )
     for load in loads:
@@ -102,6 +104,7 @@
         col = lax.broadcasted_iota(jnp.int32, (rows, width), 1)
         return jnp.logical_and(row < sizes_ref[i, 0], col < sizes_ref[i, 1])
 
+    own_load.wait()
     lives = [live(i) for i in range(2)]
     squares = jnp.zeros((8, 128), F32)
 
@@ -118,11 +121,13 @@
     def _():
         v0[0:2] = jnp.zeros((2, nz, 2, rows, width), BF16)
         v1[0:2] = jnp.zeros((2, nz, 2, rows, width), BF16)
+        th_side[0] = jnp.zeros((8, 128), F32)
 
     @pl.when(jnp.logical_not(has_hi))
     def _():
         v0[4:6] = jnp.zeros((2, nz, 2, rows, width), BF16)
         v1[4:6] = jnp.zeros((2, nz, 2, rows, width), BF16)
+        th_side[1] = jnp.zeros((8, 128), F32)
 
     pl.semaphore_wait(
         barrier,
@@ -136,21 +141,24 @@
         if nz - d != d:
             order.append(nz - d)
 
-    def gather(v):
+    def gather(v, meanwhile=None):
         zi = [sems.take() for _ in range(nz)]
         lo = [sems.take() for _ in range(nz)]
         hi = [sems.take() for _ in range(nz)]
         sib = [sems.take() for _ in range(3)]
-        mid = pl.ds(2, 2)
-        for d in order:
-            send(v.at[mid, z, c], v.at[mid, z, c], zi[d], dev(s, at_z(d), c))
+        mid, low, high = pl.ds(2, 2), pl.ds(0, 2), pl.ds(4, 2)
+        own = v.at[mid, z, c]
+        for d in reversed(order):
+            send(own, own, zi[d], dev(s, at_z(d), c))
         for d in [0] + order:
             zz = at_z(nz - d) if d else z
             block = v.at[mid, zz, c]
             if d:
                 arrive(block, zi[d])
-            send(block, v.at[pl.ds(4, 2), zz, c], lo[d], dev(s - 1, z, c), has_lo)
-            send(block, v.at[pl.ds(0, 2), zz, c], hi[d], dev(s + 1, z, c), has_hi)
+            send(block, v.at[high, zz, c], lo[d], dev(s - 1, z, c), has_lo)
+            send(block, v.at[low, zz, c], hi[d], dev(s + 1, z, c), has_hi)
+            if d == 0 and meanwhile is not None:
+                meanwhile()
         whole = [v.at[pl.ds(2 * k, 2), :, c] for k in range(3)]
         back = [v.at[pl.ds(2 * k, 2), :, other] for k in range(3)]
         send(whole[1], whole[1], sib[1], dev(s, z, other))
@@ -195,65 +203,91 @@
             acc = acc + landed[r, i, zz].astype(F32)
         return jnp.where(lives[i], acc, 0.0)
 
-    def product(r, v):
-        gather(v)
+    def product(r, v, src):
         swaps = [sems.take() for _ in range(2)]
         zis = [[sems.take() for _ in range(nz)] for _ in range(2)]
         if r == 0:
             for load in loads:
                 load.wait()
-        outs = []
-        first_half(v, 0)
-        outs.append(second_half(r, 0))
+        first_half(src, 0)
+        out = second_half(r, 0)
         swap(r, 0, swaps[0])
-        inner = fold(outs[0] * v0[2].reshape(width, width).astype(F32)) if r == 0 else None
-        first_half(v, 1)
+        if r == 0:
+            inner = fold(out * v0[2].reshape(width, width).astype(F32))
+        first_half(src, 1)
         scatter(r, 0, swaps[0], zis[0])
-        outs.append(second_half(r, 1))
+        out = second_half(r, 1)
         swap(r, 1, swaps[1])
         if r == 0:
-            inner += fold(outs[1] * v0[3].reshape(width, width).astype(F32))
+            inner += fold(out * v0[3].reshape(width, width).astype(F32))
             theta_start(inner)
         scatter(r, 1, swaps[1], zis[1])
-        theta = theta_end() if r == 0 else None
-        return [collect(r, i, zis[i]) for i in range(2)], theta
+        quotient = theta_column() if r == 0 else None
+        return [collect(r, i, zis[i]) for i in range(2)], quotient
 
     tz = [sems.take() for _ in range(n_term)]
     tx = [sems.take() for _ in range(INNER)]
     ty = [sems.take() for _ in range(n_outer)]
+    ts = [sems.take() for _ in range(2)]
+
+    def summed(own, slots, idx):
+        acc = own
+        for d in range(1, len(idx)):
+            arrive(slots.at[d], idx[d])
+            acc = acc + slots[d]
+        return acc
+
+    def ratio(both):
+        return jnp.sum(both[:4], keepdims=True) / jnp.sum(both[4:], keepdims=True)
+
+    def column_ratio(both):
+        value = ratio(both)
+        return jnp.where(jnp.abs(value) < 1e30, value, 0.0)
 
     def theta_start(inner):
         th_own[0] = jnp.concatenate([inner[:4] + inner[4:], squares[:4] + squares[4:]], axis=0)
         for d in range(1, n_term):
             send(th_own.at[0], th_z.at[d], tz[d], (s, lax.rem(t + d, n_term)))
 
-    def theta_end():
-        def summed(own, slots, idx, n):
-            acc = own
-            for d in range(1, n):
-                arrive(slots.at[d], idx[d])
-                acc = acc + slots[d]
-            return acc
-
-        th_own[1] = summed(th_own[0], th_z, tz, n_term)
+    def theta_column():
+        both = summed(th_own[0], th_z, tz)
+        th_own[1] = both
         for d in range(1, INNER):
             send(th_own.at[1], th_x.at[d], tx[d], (sy * INNER + lax.rem(sx + d, INNER), t))
-        th_own[2] = summed(th_own[1], th_x, tx, INNER)
+        send(th_own.at[1], th_side.at[1], ts[1], dev(s - 1, z, c), has_lo)
+        send(th_own.at[1], th_side.at[0], ts[0], dev(s + 1, z, c), has_hi)
+        return column_ratio(both)
+
+    def theta_across():
+        th_own[2] = summed(th_own[1], th_x, tx)
         for d in range(1, n_outer):
             send(th_own.at[2], th_y.at[d], ty[d], (lax.rem(sy + d, n_outer) * INNER + sx, t))
-        both = summed(th_own[2], th_y, ty, n_outer)
-        num = jnp.sum(both[:4], keepdims=True)
-        den = jnp.sum(both[4:], keepdims=True)
-        return num / den
-
-    sigma, theta = product(0, v0)
+
+    def theta_end():
+        theta = ratio(summed(th_own[2], th_y, ty))
+        arrive(th_side.at[0], ts[0], has_lo)
+        arrive(th_side.at[1], ts[1], has_hi)
+        return theta, column_ratio(th_side[0]), column_ratio(th_side[1])
+    gather(v0)
+    sigma, quotient = product(0, v0, v0)
     for i in range(2):
-        sigma_ref[i] = sigma[i]
+        outs[0, i] = sigma[i]
         psi = v0[2 + i, z, c].astype(F32)
-        v1[2 + i, z, c] = (sigma[i] - theta * psi).astype(BF16)
-    last, _ = product(1, v1)
+        v1[2 + i, z, c] = (sigma[i] - quotient * psi).astype(BF16)
+    sigma_out = pltpu.make_async_copy(outs.at[0], sigma_hbm, load_sem.at[0])
+    sigma_out.start()
+    gather(v1, theta_across)
+    theta, below, above = theta_end()
+    for j in range(6):
+        change = (below, quotient, above)[j // 2] - theta
+        v2[j] = (v1[j].astype(F32) + change * v0[j].astype(F32)).astype(BF16)
+    last, _ = product(1, v1, v2)
     for i in range(2):
-        next_ref[i] = last[i]
+        outs[1, i] = last[i]
+    next_out = pltpu.make_async_copy(outs.at[1], next_hbm, load_sem.at[1])
+    next_out.start()
+    sigma_out.wait()
+    next_out.wait()
     for copy, when in sent:
         if when is None:
             copy.wait_send()
@@ -269,18 +303,21 @@
         n_sector, n_term = dims
         nz = n_term // 2
         terms, width, rows = left.shape[0], left.shape[-1], psi.shape[1]
-        n_sems = 2 * (3 * nz + 3 + 2 + 2 * nz) + n_term + INNER + n_sector // INNER
+        n_sems = 2 * (3 * nz + 3 + 2 + 2 * nz) + n_term + INNER + n_sector // INNER + 2
         out = jax.ShapeDtypeStruct((2, rows, width), F32)
-        vmem, smem = (pl.BlockSpec(memory_space=m) for m in (pltpu.VMEM, pltpu.SMEM))
+        smem = pl.BlockSpec(memory_space=pltpu.SMEM)
         hbm = pl.BlockSpec(memory_space=pl.ANY)
         return pl.pallas_call(
             functools.partial(kernel, dims),
             out_shape=(out, out),
-            in_specs=[vmem, smem, smem, hbm, hbm],
-            out_specs=(vmem, vmem),
+            in_specs=[hbm, smem, smem, hbm, hbm],
+            out_specs=(hbm, hbm),
             scratch_shapes=[
+                pltpu.VMEM((2, rows, width), BF16),
+                pltpu.VMEM((2, 2, rows, width), F32),
                 pltpu.VMEM((terms, 2, width, width), BF16),
                 pltpu.VMEM((2, width, terms * width), BF16),
+                pltpu.VMEM((6, nz, 2, rows, width), BF16),
                 pltpu.VMEM((6, nz, 2, rows, width), BF16),
                 pltpu.VMEM((6, nz, 2, rows, width), BF16),
                 pltpu.VMEM((width, terms * width), BF16),
@@ -292,7 +329,8 @@
                 pltpu.VMEM((n_term, 8, 128), F32),
                 pltpu.VMEM((INNER, 8, 128), F32),
                 pltpu.VMEM((n_sector // INNER, 8, 128), F32),
-                pltpu.SemaphoreType.DMA((1 + 2 * terms,)),
+                pltpu.VMEM((2, 8, 128), F32),
+                pltpu.SemaphoreType.DMA((2 + 2 * terms,)),
                 pltpu.SemaphoreType.DMA((n_sems,)),
                 pltpu.SemaphoreType.DMA((n_sems,)),
             ],

time: 69.8 us -> 61.7 us (0.88)
  the two profiles are of different devices: /device:TPU:9 before, /device:TPU:7 now
where the time goes in v2:
time: 61.7 us; the launch traced here: 61.5 us
  Pallas kernels  58.1 us (94%)
  local copies, waits for them, and re-layouts  2.75 us (4%)
  between operations  0.64 us (1%)
    pallas_call x1, Pallas kernels, step(): pl.pallas_call(functools.partial(kernel, dims), out_shape=(out, out), in_...  58.1 us
    unnamed x2, local copies, waits for them, and re-layouts  2.75 us

profile of v2, /device:TPU:7, one launch (start us, length us, event | category | flops | bytes accessed | tf_op | source)
XLA Modules:
  0.0 61.5 jit_solution(18313984835249769056)
XLA Ops:
  0.6 58.1 %shard_map.68 = (f32[2,16,256]{2,1,0:T(8,128)}, f32[2,16,256]{2,1,0:T(8,128)}) custom-call(bf16[2,16,256]{2,1,0:T(8,128)(2,1)} %psi_hbm.1, s32[2,2]{1,0:T(2,128)} %sizes_ref.1, s32[8]{0:T(128)} %shifts_ref.1, bf16[8,2,256,256]{3,2,1,0:T(8,128)(2,1)} %left_hbm.1, bf16[8,2,256,256]{3,2,1,0:T(8,128)(2,1)} %right_hbm.1), custom_call_target="tpu_custom_call" | custom-call | flops 2147483648 | bytes 4194304 | tf_op jit(solution)/shard_map/pallas_call | solution.py:310
  58.7 1.4 %copy.9 = f32[2,16,256]{2,1,0:T(8,128)} copy(f32[2,16,256]{2,1,0:T(8,128)} %get-tuple-element.4) | data formatting | bytes 65536
  60.1 1.4 %copy.10 = f32[2,16,256]{2,1,0:T(8,128)} copy(f32[2,16,256]{2,1,0:T(8,128)} %get-tuple-element.5) | data formatting | bytes 65536

commit v3 on v2

--- a/solution.py
+++ b/solution.py
@@ -14,12 +14,12 @@
 
 
 class Sems:
-    def __init__(self, send, recv):
-        self.send, self.recv, self.count = send, recv, 0
+    def __init__(self, sems):
+        self.sems, self.count = sems, 0
 
     def take(self):
         self.count += 1
-        return self.count - 1
+        return self.sems.at[self.count - 1]
 
 
 def kernel(
@@ -37,7 +37,7 @@
     sx, sy = s % INNER, s // INNER
     other = 1 - c
     has_lo, has_hi = s > 0, s < n_sector - 1
-    sems = Sems(send_sem, recv_sem)
+    sends, recvs = Sems(send_sem), Sems(recv_sem)
     sent = []
 
     def at_z(d):
@@ -46,41 +46,39 @@
     def dev(sector, zz, core):
         return (sector, zz * 2 + core)
 
-    def remote(src, dst, idx, device):
+    def guarded(when, act):
+        if when is None:
+            act()
+        else:
+            pl.when(when)(act)
+
+    def remote(src, dst, out_sem, in_sem, device):
         return pltpu.make_async_remote_copy(
-            src_ref=src, dst_ref=dst, send_sem=send_sem.at[idx], recv_sem=recv_sem.at[idx],
+            src_ref=src, dst_ref=dst, send_sem=out_sem, recv_sem=in_sem,
             device_id=device, device_id_type=MESH,
         )
 
-    def send(src, dst, idx, device, when=None):
-        copy = remote(src, dst, idx, device)
-        if when is None:
-            copy.start()
-        else:
-            pl.when(when)(copy.start)
-        sent.append((copy, when))
-
-    def arrive(dst, idx, when=None):
-        copy = remote(dst, dst, idx, dev(s, z, other))
-        if when is None:
-            copy.wait_recv()
-        else:
-            pl.when(when)(copy.wait_recv)
+    def send(src, dst, group, device):
+        out_sem, in_sem, when = group
+        guarded(when, remote(src, dst, out_sem, in_sem, device).start)
+
+    def group(region, when=None):
+        out_sem, in_sem = sends.take(), recvs.take()
+        sent.append((remote(region, region, out_sem, in_sem, dev(s, z, other)), when))
+        return out_sem, in_sem, when
+
+    def arrive(region, in_sem, when=None):
+        copy = remote(region, region, send_sem.at[0], in_sem, dev(s, z, other))
+        guarded(when, copy.wait_recv)
 
     own_load = pltpu.make_async_copy(psi_hbm, psi_ref, load_sem.at[0])
     own_load.start()
-    loads = []
-    loads.append(pltpu.make_async_copy(left_hbm, left, load_sem.at[1]))
+    pltpu.make_async_copy(left_hbm, left, load_sem.at[1]).start()
     for k in range(terms):
         for i in range(2):
-            loads.append(
-                pltpu.make_async_copy(
-                    right_hbm.at[k, i], right.at[i, :, pl.ds(k * width, width)],
-                    load_sem.at[2 + 2 * k + i],
-                )
-            )
-    for load in loads:
-        load.start()
+            pltpu.make_async_copy(
+                right_hbm.at[k, i], right.at[i, :, pl.ds(k * width, width)], load_sem.at[2]
+            ).start()
 
     barrier = pltpu.get_barrier_semaphore()
 
@@ -141,36 +139,37 @@
         if nz - d != d:
             order.append(nz - d)
 
+    mid, low, high = pl.ds(2, 2), pl.ds(0, 2), pl.ds(4, 2)
+    most = pl.ds(0, nz - 1)
+
     def gather(v, meanwhile=None):
-        zi = [sems.take() for _ in range(nz)]
-        lo = [sems.take() for _ in range(nz)]
-        hi = [sems.take() for _ in range(nz)]
-        sib = [sems.take() for _ in range(3)]
-        mid, low, high = pl.ds(2, 2), pl.ds(0, 2), pl.ds(4, 2)
+        along = group(v.at[mid, most, c])
+        along_in = {d: recvs.take() for d in order}
+        down = group(v.at[mid, :, c], has_lo)
+        up = group(v.at[mid, :, c], has_hi)
+        pair = group(v.at[mid, :, c])
+        pair_low = group(v.at[low, :, c], has_lo)
+        pair_high = group(v.at[high, :, c], has_hi)
         own = v.at[mid, z, c]
         for d in reversed(order):
-            send(own, own, zi[d], dev(s, at_z(d), c))
+            send(own, own, (along[0], along_in[d], None), dev(s, at_z(d), c))
         for d in [0] + order:
             zz = at_z(nz - d) if d else z
             block = v.at[mid, zz, c]
             if d:
-                arrive(block, zi[d])
-            send(block, v.at[high, zz, c], lo[d], dev(s - 1, z, c), has_lo)
-            send(block, v.at[low, zz, c], hi[d], dev(s + 1, z, c), has_hi)
+                arrive(block, along_in[d])
+            send(block, v.at[high, zz, c], down, dev(s - 1, z, c))
+            send(block, v.at[low, zz, c], up, dev(s + 1, z, c))
+            send(block, block, pair, dev(s, z, other))
             if d == 0 and meanwhile is not None:
                 meanwhile()
-        whole = [v.at[pl.ds(2 * k, 2), :, c] for k in range(3)]
-        back = [v.at[pl.ds(2 * k, 2), :, other] for k in range(3)]
-        send(whole[1], whole[1], sib[1], dev(s, z, other))
-        for d in [0] + order:
-            zz = at_z(nz - d) if d else z
-            arrive(v.at[pl.ds(0, 2), zz, c], hi[d], has_lo)
-            arrive(v.at[pl.ds(4, 2), zz, c], lo[d], has_hi)
-        send(whole[0], whole[0], sib[0], dev(s, z, other), has_lo)
-        send(whole[2], whole[2], sib[2], dev(s, z, other), has_hi)
-        arrive(back[1], sib[1])
-        arrive(back[0], sib[0], has_lo)
-        arrive(back[2], sib[2], has_hi)
+        arrive(v.at[low, :, c], up[1], has_lo)
+        send(v.at[low, :, c], v.at[low, :, c], pair_low, dev(s, z, other))
+        arrive(v.at[high, :, c], down[1], has_hi)
+        send(v.at[high, :, c], v.at[high, :, c], pair_high, dev(s, z, other))
+        arrive(v.at[mid, :, other], pair[1])
+        arrive(v.at[low, :, other], pair_low[1], has_lo)
+        arrive(v.at[high, :, other], pair_high[1], has_hi)
 
     def first_half(v, i):
         for k in range(terms):
@@ -185,57 +184,55 @@
         total[r, i] = out.reshape(nz, 2, rows, width)
         return out
 
-    def swap(r, i, idx):
-        send(total.at[r, i, :, other], peer.at[r, i], idx, dev(s, z, other))
-
-    def scatter(r, i, idx, zi):
-        arrive(peer.at[r, i], idx)
+    def swap(r, i):
+        pair = group(total.at[r, i, :, other])
+        send(total.at[r, i, :, other], peer.at[r, i], pair, dev(s, z, other))
+        return pair
+
+    def scatter(r, i, pair, along):
+        arrive(peer.at[r, i], pair[1])
         chunk[r, i] = (total[r, i, :, c] + peer[r, i]).astype(chunk.dtype)
-        for d in order:
+        for d in reversed(order):
             zz = at_z(d)
-            send(chunk.at[r, i, zz], landed.at[r, i, z], zi[d], dev(s, zz, c))
-
-    def collect(r, i, zi):
+            send(chunk.at[r, i, zz], landed.at[r, i, z], along, dev(s, zz, c))
+
+    def collect(r, i):
         acc = total[r, i, z, c] + peer[r, i, z]
         for d in order:
-            zz = at_z(nz - d)
-            arrive(landed.at[r, i, zz], zi[d])
-            acc = acc + landed[r, i, zz].astype(F32)
+            acc = acc + landed[r, i, at_z(nz - d)].astype(F32)
         return jnp.where(lives[i], acc, 0.0)
 
     def product(r, v, src):
-        swaps = [sems.take() for _ in range(2)]
-        zis = [[sems.take() for _ in range(nz)] for _ in range(2)]
+        along = group(chunk.at[r, :, most])
         if r == 0:
-            for load in loads:
-                load.wait()
+            pltpu.make_async_copy(left_hbm, left, load_sem.at[1]).wait()
+            pltpu.make_async_copy(right, right, load_sem.at[2]).wait()
         first_half(src, 0)
         out = second_half(r, 0)
-        swap(r, 0, swaps[0])
+        first = swap(r, 0)
         if r == 0:
             inner = fold(out * v0[2].reshape(width, width).astype(F32))
         first_half(src, 1)
-        scatter(r, 0, swaps[0], zis[0])
+        scatter(r, 0, first, along)
         out = second_half(r, 1)
-        swap(r, 1, swaps[1])
+        second = swap(r, 1)
         if r == 0:
             inner += fold(out * v0[3].reshape(width, width).astype(F32))
             theta_start(inner)
-        scatter(r, 1, swaps[1], zis[1])
+        scatter(r, 1, second, along)
         quotient = theta_column() if r == 0 else None
-        return [collect(r, i, zis[i]) for i in range(2)], quotient
-
-    tz = [sems.take() for _ in range(n_term)]
-    tx = [sems.take() for _ in range(INNER)]
-    ty = [sems.take() for _ in range(n_outer)]
-    ts = [sems.take() for _ in range(2)]
-
-    def summed(own, slots, idx):
-        acc = own
-        for d in range(1, len(idx)):
-            arrive(slots.at[d], idx[d])
-            acc = acc + slots[d]
-        return acc
+        arrive(landed.at[r, :, most], along[1])
+        return [collect(r, i) for i in range(2)], quotient
+
+    th_column = group(th_z.at[pl.ds(1, n_term - 1)])
+    th_inner = group(th_x.at[pl.ds(1, INNER - 1)])
+    th_outer = group(th_y.at[pl.ds(1, n_outer - 1)])
+    th_down, th_up = group(th_own.at[1], has_lo), group(th_own.at[1], has_hi)
+
+    def summed(own, slots, incoming):
+        n = slots.shape[0]
+        arrive(slots.at[pl.ds(1, n - 1)], incoming[1])
+        return functools.reduce(jnp.add, [slots[d] for d in range(1, n)], own)
 
     def ratio(both):
         return jnp.sum(both[:4], keepdims=True) / jnp.sum(both[4:], keepdims=True)
@@ -247,26 +244,26 @@
     def theta_start(inner):
         th_own[0] = jnp.concatenate([inner[:4] + inner[4:], squares[:4] + squares[4:]], axis=0)
         for d in range(1, n_term):
-            send(th_own.at[0], th_z.at[d], tz[d], (s, lax.rem(t + d, n_term)))
+            send(th_own.at[0], th_z.at[d], th_column, (s, lax.rem(t + d, n_term)))
 
     def theta_column():
-        both = summed(th_own[0], th_z, tz)
+        both = summed(th_own[0], th_z, th_column)
         th_own[1] = both
         for d in range(1, INNER):
-            send(th_own.at[1], th_x.at[d], tx[d], (sy * INNER + lax.rem(sx + d, INNER), t))
-        send(th_own.at[1], th_side.at[1], ts[1], dev(s - 1, z, c), has_lo)
-        send(th_own.at[1], th_side.at[0], ts[0], dev(s + 1, z, c), has_hi)
+            send(th_own.at[1], th_x.at[d], th_inner, (sy * INNER + lax.rem(sx + d, INNER), t))
+        send(th_own.at[1], th_side.at[1], th_down, dev(s - 1, z, c))
+        send(th_own.at[1], th_side.at[0], th_up, dev(s + 1, z, c))
         return column_ratio(both)
 
     def theta_across():
-        th_own[2] = summed(th_own[1], th_x, tx)
+        th_own[2] = summed(th_own[1], th_x, th_inner)
         for d in range(1, n_outer):
-            send(th_own.at[2], th_y.at[d], ty[d], (lax.rem(sy + d, n_outer) * INNER + sx, t))
+            send(th_own.at[2], th_y.at[d], th_outer, (lax.rem(sy + d, n_outer) * INNER + sx, t))
 
     def theta_end():
-        theta = ratio(summed(th_own[2], th_y, ty))
-        arrive(th_side.at[0], ts[0], has_lo)
-        arrive(th_side.at[1], ts[1], has_hi)
+        theta = ratio(summed(th_own[2], th_y, th_outer))
+        arrive(th_side.at[0], th_up[1], has_lo)
+        arrive(th_side.at[1], th_down[1], has_hi)
         return theta, column_ratio(th_side[0]), column_ratio(th_side[1])
     gather(v0)
     sigma, quotient = product(0, v0, v0)
@@ -289,11 +286,7 @@
     sigma_out.wait()
     next_out.wait()
     for copy, when in sent:
-        if when is None:
-            copy.wait_send()
-        else:
-            pl.when(when)(copy.wait_send)
-    assert sems.count <= send_sem.shape[0]
+        guarded(when, copy.wait_send)
 
 
 def solution(mesh, link=BF16):
@@ -303,7 +296,7 @@
         n_sector, n_term = dims
         nz = n_term // 2
         terms, width, rows = left.shape[0], left.shape[-1], psi.shape[1]
-        n_sems = 2 * (3 * nz + 3 + 2 + 2 * nz) + n_term + INNER + n_sector // INNER + 2
+        n_send, n_recv = 2 * 9 + 5, 2 * (9 + nz - 1) + 5
         out = jax.ShapeDtypeStruct((2, rows, width), F32)
         smem = pl.BlockSpec(memory_space=pltpu.SMEM)
         hbm = pl.BlockSpec(memory_space=pl.ANY)
@@ -330,9 +323,9 @@
                 pltpu.VMEM((INNER, 8, 128), F32),
                 pltpu.VMEM((n_sector // INNER, 8, 128), F32),
                 pltpu.VMEM((2, 8, 128), F32),
-                pltpu.SemaphoreType.DMA((2 + 2 * terms,)),
-                pltpu.SemaphoreType.DMA((n_sems,)),
-                pltpu.SemaphoreType.DMA((n_sems,)),
+                pltpu.SemaphoreType.DMA((3,)),
+                pltpu.SemaphoreType.DMA((n_send,)),
+                pltpu.SemaphoreType.DMA((n_recv,)),
             ],
             compiler_params=pltpu.CompilerParams(
                 collective_id=0, has_side_effects=True, vmem_limit_bytes=62 * 2**20

time: 61.7 us -> 58.9 us (0.955)
  Pallas kernels: 58.1 us -> 55.2 us
    pallas_call x1, Pallas kernels: 58.1 us -> 55.2 us  [step(): pl.pallas_call(functools.partial(kernel, dims), out_shape=(out, out), in_...]
where the time goes in v3:
time: 58.9 us; the launch traced here: 58.6 us
  Pallas kernels  55.2 us (94%)
  local copies, waits for them, and re-layouts  2.75 us (5%)
  between operations  0.64 us (1%)
    pallas_call x1, Pallas kernels, step(): pl.pallas_call(functools.partial(kernel, dims), out_shape=(out, out), in_...  55.2 us
    unnamed x2, local copies, waits for them, and re-layouts  2.75 us

profile of v3, /device:TPU:7, one launch (start us, length us, event | category | flops | bytes accessed | tf_op | source)
XLA Modules:
  0.0 58.6 jit_solution(4588496252569472694)
XLA Ops:
  0.6 55.2 %shard_map.68 = (f32[2,16,256]{2,1,0:T(8,128)}, f32[2,16,256]{2,1,0:T(8,128)}) custom-call(bf16[2,16,256]{2,1,0:T(8,128)(2,1)} %psi_hbm.1, s32[2,2]{1,0:T(2,128)} %sizes_ref.1, s32[8]{0:T(128)} %shifts_ref.1, bf16[8,2,256,256]{3,2,1,0:T(8,128)(2,1)} %left_hbm.1, bf16[8,2,256,256]{3,2,1,0:T(8,128)(2,1)} %right_hbm.1), custom_call_target="tpu_custom_call" | custom-call | flops 2147483648 | bytes 4194304 | tf_op jit(solution)/shard_map/pallas_call | solution.py:303
  55.8 1.4 %copy.9 = f32[2,16,256]{2,1,0:T(8,128)} copy(f32[2,16,256]{2,1,0:T(8,128)} %get-tuple-element.4) | data formatting | bytes 65536
  57.2 1.4 %copy.10 = f32[2,16,256]{2,1,0:T(8,128)} copy(f32[2,16,256]{2,1,0:T(8,128)} %get-tuple-element.5) | data formatting | bytes 65536

commit v4 on v3

--- a/solution.py
+++ b/solution.py
@@ -23,8 +23,8 @@
 
 
 def kernel(
-    dims, psi_hbm, sizes_ref, shifts_ref, left_hbm, right_hbm, sigma_hbm, next_hbm,
-    psi_ref, outs, left, right, v0, v1, v2, mixed, total, peer, chunk, landed,
+    dims, psi_hbm, sizes_hbm, shifts_hbm, left_hbm, right_hbm, out_hbm,
+    psi_ref, sizes_ref, shifts_ref, outs, left, right, v0, v1, v2, mixed, total, peer, chunk, landed,
     th_own, th_z, th_x, th_y, th_side, load_sem, send_sem, recv_sem,
 ):
     n_sector, n_term = dims
@@ -73,6 +73,10 @@
 
     own_load = pltpu.make_async_copy(psi_hbm, psi_ref, load_sem.at[0])
     own_load.start()
+    sizes_load = pltpu.make_async_copy(sizes_hbm, sizes_ref, load_sem.at[3])
+    shifts_load = pltpu.make_async_copy(shifts_hbm, shifts_ref, load_sem.at[4])
+    sizes_load.start()
+    shifts_load.start()
     pltpu.make_async_copy(left_hbm, left, load_sem.at[1]).start()
     for k in range(terms):
         for i in range(2):
@@ -102,6 +106,8 @@
         col = lax.broadcasted_iota(jnp.int32, (rows, width), 1)
         return jnp.logical_and(row < sizes_ref[i, 0], col < sizes_ref[i, 1])
 
+    sizes_load.wait()
+    shifts_load.wait()
     own_load.wait()
     lives = [live(i) for i in range(2)]
     squares = jnp.zeros((8, 128), F32)
@@ -271,7 +277,7 @@
         outs[0, i] = sigma[i]
         psi = v0[2 + i, z, c].astype(F32)
         v1[2 + i, z, c] = (sigma[i] - quotient * psi).astype(BF16)
-    sigma_out = pltpu.make_async_copy(outs.at[0], sigma_hbm, load_sem.at[0])
+    sigma_out = pltpu.make_async_copy(outs.at[0], out_hbm.at[0], load_sem.at[0])
     sigma_out.start()
     gather(v1, theta_across)
     theta, below, above = theta_end()
@@ -281,7 +287,7 @@
     last, _ = product(1, v1, v2)
     for i in range(2):
         outs[1, i] = last[i]
-    next_out = pltpu.make_async_copy(outs.at[1], next_hbm, load_sem.at[1])
+    next_out = pltpu.make_async_copy(outs.at[1], out_hbm.at[1], load_sem.at[1])
     next_out.start()
     sigma_out.wait()
     next_out.wait()
@@ -297,16 +303,17 @@
         nz = n_term // 2
         terms, width, rows = left.shape[0], left.shape[-1], psi.shape[1]
         n_send, n_recv = 2 * 9 + 5, 2 * (9 + nz - 1) + 5
-        out = jax.ShapeDtypeStruct((2, rows, width), F32)
-        smem = pl.BlockSpec(memory_space=pltpu.SMEM)
+        out = jax.ShapeDtypeStruct((2, 2, rows, width), F32)
         hbm = pl.BlockSpec(memory_space=pl.ANY)
-        return pl.pallas_call(
+        both = pl.pallas_call(
             functools.partial(kernel, dims),
-            out_shape=(out, out),
-            in_specs=[hbm, smem, smem, hbm, hbm],
-            out_specs=(hbm, hbm),
+            out_shape=out,
+            in_specs=[hbm] * 5,
+            out_specs=hbm,
             scratch_shapes=[
                 pltpu.VMEM((2, rows, width), BF16),
+                pltpu.SMEM((2, 2), jnp.int32),
+                pltpu.SMEM((terms,), jnp.int32),
                 pltpu.VMEM((2, 2, rows, width), F32),
                 pltpu.VMEM((terms, 2, width, width), BF16),
                 pltpu.VMEM((2, width, terms * width), BF16),
@@ -323,7 +330,7 @@
                 pltpu.VMEM((INNER, 8, 128), F32),
                 pltpu.VMEM((n_sector // INNER, 8, 128), F32),
                 pltpu.VMEM((2, 8, 128), F32),
-                pltpu.SemaphoreType.DMA((3,)),
+                pltpu.SemaphoreType.DMA((5,)),
                 pltpu.SemaphoreType.DMA((n_send,)),
                 pltpu.SemaphoreType.DMA((n_recv,)),
             ],
@@ -335,6 +342,7 @@
                 transcendentals=0,
             ),
         )(psi, sizes, shifts, left, right)
+        return both[0], both[1]
 
     return jax.shard_map(
         step,

time: 58.9 us -> 56.9 us (0.966)
  local copies, waits for them, and re-layouts: 2.75 us -> 1.41 us
  Pallas kernels: 55.2 us -> 54.5 us
    unnamed x2 -> x0, local copies, waits for them, and re-layouts: 2.75 us -> none
    squeeze x0 -> x1, local copies, waits for them, and re-layouts: none -> 1.41 us  [step(): return (both[0], both[1])]
    pallas_call x1, Pallas kernels: 55.2 us -> 54.5 us  [step(): pl.pallas_call(functools.partial(kernel, dims), out_shape=out, in_specs=[...]
where the time goes in v4:
time: 56.9 us; the launch traced here: 56.6 us
  Pallas kernels  54.5 us (96%)
  local copies, waits for them, and re-layouts  1.41 us (2%)
  between operations  0.64 us (1%)
    pallas_call x1, Pallas kernels, step(): pl.pallas_call(functools.partial(kernel, dims), out_shape=out, in_specs=[...  54.5 us
    squeeze x1, local copies, waits for them, and re-layouts, step(): return (both[0], both[1])  1.41 us

profile of v4, /device:TPU:7, one launch (start us, length us, event | category | flops | bytes accessed | tf_op | source)
XLA Modules:
  0.0 56.6 jit_solution(3611330831917571332)
XLA Ops:
  0.6 54.5 %shard_map.68 = f32[2,2,16,256]{3,2,1,0:T(8,128)} custom-call(bf16[2,16,256]{2,1,0:T(8,128)(2,1)} %psi_hbm.1, s32[2,2]{1,0:T(2,128)} %sizes_hbm.1, s32[8]{0:T(128)} %shifts_hbm.1, bf16[8,2,256,256]{3,2,1,0:T(8,128)(2,1)} %left_hbm.1, bf16[8,2,256,256]{3,2,1,0:T(8,128)(2,1)} %right_hbm.1), custom_call_target="tpu_custom_call" | custom-call | flops 2147483648 | bytes 4194304 | tf_op jit(solution)/shard_map/pallas_call | solution.py:308
  55.2 1.4 %slice_bitcast_fusion = (f32[2,16,256]{2,1,0:T(8,128)}, f32[2,16,256]{2,1,0:T(8,128)}) fusion(f32[2,2,16,256]{3,2,1,0:T(8,128)} %shard_map.68), kind=kLoop, calls=%fused_computation | loop fusion | bytes 131072 | tf_op jit(solution)/shard_map/squeeze | solution.py:345

commit v5 on v4

--- a/solution.py
+++ b/solution.py
@@ -100,6 +100,8 @@
     hi_cross = jnp.logical_and(has_hi, sx == INNER - 1)
     pl.when(lo_cross)(lambda: greet(dev(s - 1, z, c)))
     pl.when(hi_cross)(lambda: greet(dev(s + 1, z, c)))
+    pl.when(has_lo)(lambda: greet(dev(s - 1, z, other)))
+    pl.when(has_hi)(lambda: greet(dev(s + 1, z, other)))
 
     def live(i):
         row = lax.broadcasted_iota(jnp.int32, (rows, width), 0) + t * rows
@@ -136,7 +138,8 @@
     pl.semaphore_wait(
         barrier,
         1 + (nz - 1) + (INNER - 1) + (n_outer - 1)
-        + lo_cross.astype(jnp.int32) + hi_cross.astype(jnp.int32),
+        + lo_cross.astype(jnp.int32) + hi_cross.astype(jnp.int32)
+        + has_lo.astype(jnp.int32) + has_hi.astype(jnp.int32),
     )
 
     order = []
@@ -151,31 +154,53 @@
     def gather(v, meanwhile=None):
         along = group(v.at[mid, most, c])
         along_in = {d: recvs.take() for d in order}
-        down = group(v.at[mid, :, c], has_lo)
-        up = group(v.at[mid, :, c], has_hi)
+        near = [d for d in [0] + order if min(d, nz - d) < nz // 2 - 1]
+        far = [d for d in order if d not in near]
+        few, many = pl.ds(0, len(far)), pl.ds(0, len(near))
         pair = group(v.at[mid, :, c])
-        pair_low = group(v.at[low, :, c], has_lo)
-        pair_high = group(v.at[high, :, c], has_hi)
+        sides = []
+        for to, step, when_out, when_in in (
+            (high, -1, has_lo, has_hi), (low, 1, has_hi, has_lo),
+        ):
+            sides.append((
+                to, step, when_in,
+                group(v.at[mid, many, c], when_out), group(v.at[mid, few, c], when_out),
+                group(v.at[mid, few, c], when_out), group(v.at[to, many, c], when_in),
+            ))
         own = v.at[mid, z, c]
         for d in reversed(order):
             send(own, own, (along[0], along_in[d], None), dev(s, at_z(d), c))
-        for d in [0] + order:
-            zz = at_z(nz - d) if d else z
-            block = v.at[mid, zz, c]
+
+        def place(d):
+            return at_z(nz - d) if d else z
+
+        def cross():
+            for to, _, when_in, narrow, _, _, shared in sides:
+                arrive(v.at[to, many, c], narrow[1], when_in)
+                for d in near:
+                    block = v.at[to, place(d), c]
+                    send(block, block, shared, dev(s, z, other))
+
+        for d in near + far:
+            block = v.at[mid, place(d), c]
             if d:
                 arrive(block, along_in[d])
-            send(block, v.at[high, zz, c], down, dev(s - 1, z, c))
-            send(block, v.at[low, zz, c], up, dev(s + 1, z, c))
+            for to, step, _, narrow, same, across, _ in sides:
+                target = v.at[to, place(d), c]
+                if d in near:
+                    send(block, target, narrow, dev(s + step, z, c))
+                else:
+                    send(block, target, same, dev(s + step, z, c))
+                    send(block, target, across, dev(s + step, z, other))
             send(block, block, pair, dev(s, z, other))
             if d == 0 and meanwhile is not None:
                 meanwhile()
-        arrive(v.at[low, :, c], up[1], has_lo)
-        send(v.at[low, :, c], v.at[low, :, c], pair_low, dev(s, z, other))
-        arrive(v.at[high, :, c], down[1], has_hi)
-        send(v.at[high, :, c], v.at[high, :, c], pair_high, dev(s, z, other))
+        cross()
         arrive(v.at[mid, :, other], pair[1])
-        arrive(v.at[low, :, other], pair_low[1], has_lo)
-        arrive(v.at[high, :, other], pair_high[1], has_hi)
+        for to, _, when_in, _, same, across, shared in sides:
+            arrive(v.at[to, many, other], shared[1], when_in)
+            arrive(v.at[to, few, c], same[1], when_in)
+            arrive(v.at[to, few, other], across[1], when_in)
 
     def first_half(v, i):
         for k in range(terms):
@@ -302,7 +327,7 @@
         n_sector, n_term = dims
         nz = n_term // 2
         terms, width, rows = left.shape[0], left.shape[-1], psi.shape[1]
-        n_send, n_recv = 2 * 9 + 5, 2 * (9 + nz - 1) + 5
+        n_send, n_recv = 2 * 13 + 5, 2 * (13 + nz - 1) + 5
         out = jax.ShapeDtypeStruct((2, 2, rows, width), F32)
         hbm = pl.BlockSpec(memory_space=pl.ANY)
         both = pl.pallas_call(

time: 56.9 us -> 56.4 us (level)
  Pallas kernels: 54.5 us -> 53.7 us
    pallas_call x1, Pallas kernels: 54.5 us -> 53.7 us  [step(): pl.pallas_call(functools.partial(kernel, dims), out_shape=out, in_specs=[...]
where the time goes in v5:
time: 56.4 us; the launch traced here: 55.7 us
  Pallas kernels  53.7 us (95%)
  local copies, waits for them, and re-layouts  1.41 us (2%)
  between operations  0.64 us (1%)
    pallas_call x1, Pallas kernels, step(): pl.pallas_call(functools.partial(kernel, dims), out_shape=out, in_specs=[...  53.7 us
    squeeze x1, local copies, waits for them, and re-layouts, step(): return (both[0], both[1])  1.41 us

profile of v5, /device:TPU:7, one launch (start us, length us, event | category | flops | bytes accessed | tf_op | source)
XLA Modules:
  0.0 55.7 jit_solution(7867060181679985944)
XLA Ops:
  0.6 53.7 %shard_map.68 = f32[2,2,16,256]{3,2,1,0:T(8,128)} custom-call(bf16[2,16,256]{2,1,0:T(8,128)(2,1)} %psi_hbm.1, s32[2,2]{1,0:T(2,128)} %sizes_hbm.1, s32[8]{0:T(128)} %shifts_hbm.1, bf16[8,2,256,256]{3,2,1,0:T(8,128)(2,1)} %left_hbm.1, bf16[8,2,256,256]{3,2,1,0:T(8,128)(2,1)} %right_hbm.1), custom_call_target="tpu_custom_call" | custom-call | flops 2147483648 | bytes 4194304 | tf_op jit(solution)/shard_map/pallas_call | solution.py:333
  54.3 1.4 %slice_bitcast_fusion = (f32[2,16,256]{2,1,0:T(8,128)}, f32[2,16,256]{2,1,0:T(8,128)}) fusion(f32[2,2,16,256]{3,2,1,0:T(8,128)} %shard_map.68), kind=kLoop, calls=%fused_computation | loop fusion | bytes 131072 | tf_op jit(solution)/shard_map/squeeze | solution.py:370
